TPU v7x, 32 devices: a whole 2x2x4 slice. The times are simulated.
32 devices in a mesh: tile: 4 (over y, core), rep: 8 (over z, x).
Axes of the slice: x: 2, y: 2, z: 4, core: 2. Of those that a mesh axis runs over, the one named last changes fastest.
Arguments:
- inputs: bfloat16 [8, 8, 32, 32, 256], P('rep', 'tile'), may hold values from -6 to 6
- grad_out: bfloat16 [8, 8, 32, 32, 256], P('rep', 'tile'), may hold values from -6 to 6
- seam_links: int32 [8, 4, 3], P('tile'), may hold values from 0 to 7, as said below
- corner_links: int32 [8, 4, 2], P('tile'), may hold values from 0 to 7, as said below
- dw_weight: float32 [256, 9], replicated, may hold values from -1 to 1
- norm_gain: float32 [256], replicated, may hold values from 0.1 to 1.9
- w_in: bfloat16 [256, 1024], replicated, may hold values from -0.375 to 0.375
- bias_in: float32 [1024], replicated, may hold values from -1 to 1
- w_out: bfloat16 [1024, 256], replicated, may hold values from -0.1875 to 0.1875
- layer_scale: float32 [256], replicated, may hold values from 0.25 to 2
Outputs:
- block_out: bfloat16 [8, 8, 32, 32, 256], P('rep', 'tile')
- x_grad: float32 [8, 8, 32, 32, 256], P('rep', 'tile')
- grad_dw: float32 [256, 9], replicated
- grad_gain: float32 [256], replicated
- grad_w_in: float32 [256, 1024], replicated
- grad_bias: float32 [1024], replicated
- grad_w_out: float32 [1024, 256], replicated
- grad_scale: float32 [256], replicated
Inputs may be any that keep to these rules, and one draw needn't show every extreme that they name: `seam_links`: entry [t, s] = (t2, s2, f): side s of tile t meets side s2 of tile t2, reversed if f = 1. Sides are paired: entry [t2, s2] = (t, s, f), and no entry names its own side. `corner_links`: entry [t, k] = (t2, k2): corner k of tile t meets corner k2 of tile t2. Corners are paired: entry [t2, k2] = (t, k), and no entry names its own corner.
All inputs are finite; a program needn't handle non-finite values.
Results may differ from a plain program's by a relative error of at most 0.0063.
Values may be sent and summed in bfloat16 or wider, within the bound.
A program may use at most 64 MiB of HBM per device.

v0:
```python
import math
import jax
import jax.numpy as jnp
from jax import lax
from jax.sharding import PartitionSpec as P

INV_ROOT_TWO = 0.7071067811865476
INV_ROOT_TAU = 0.3989422804014327


def edge_strips(blocks):
    top_row = blocks[..., 0, :, :]
    right_col = blocks[..., :, -1, :]
    bottom_row = blocks[..., -1, ::-1, :]
    left_col = blocks[..., ::-1, 0, :]
    return jnp.stack([top_row, right_col, bottom_row, left_col], axis=-3)


def corner_cells(blocks):
    return jnp.stack(
        [
            blocks[..., 0, 0, :],
            blocks[..., 0, -1, :],
            blocks[..., -1, -1, :],
            blocks[..., -1, 0, :],
        ],
        axis=-2,
    )


def fetch_linked(all_strips, all_points, seam_links, corner_links):
    picked = all_strips[:, seam_links[..., 0], seam_links[..., 1]]
    reverse = (seam_links[..., 2] == 1)[None, :, :, None, None]
    strips = jnp.where(reverse, picked[..., ::-1, :], picked)
    points = all_points[:, corner_links[..., 0], corner_links[..., 1]]
    return (strips, points)


def assemble(blocks, strips, points):
    top_row = jnp.concatenate(
        [points[..., 0:1, :], strips[..., 0, :, :], points[..., 1:2, :]], axis=-2
    )
    bottom_row = jnp.concatenate(
        [points[..., 3:4, :], strips[..., 2, ::-1, :], points[..., 2:3, :]], axis=-2
    )
    left_col = strips[..., 3, ::-1, :][..., :, None, :]
    right_col = strips[..., 1, :, :][..., :, None, :]
    middle = jnp.concatenate([left_col, blocks, right_col], axis=-2)
    return jnp.concatenate([top_row[..., None, :, :], middle, bottom_row[..., None, :, :]], axis=-3)


def padded_parts(grad_padded):
    interior = grad_padded[..., 1:-1, 1:-1, :]
    top_row = grad_padded[..., 0, 1:-1, :]
    right_col = grad_padded[..., 1:-1, -1, :]
    bottom_row = grad_padded[..., -1, 1:-1, :][..., ::-1, :]
    left_col = grad_padded[..., 1:-1, 0, :][..., ::-1, :]
    strips = jnp.stack([top_row, right_col, bottom_row, left_col], axis=-3)
    points = jnp.stack(
        [
            grad_padded[..., 0, 0, :],
            grad_padded[..., 0, -1, :],
            grad_padded[..., -1, -1, :],
            grad_padded[..., -1, 0, :],
        ],
        axis=-2,
    )
    return (interior, strips, points)


def add_to_rims(target, strips, points):
    extent = target.shape[-2]
    row_ids = lax.broadcasted_iota(jnp.int32, (extent, 1, 1), 0)
    col_ids = lax.broadcasted_iota(jnp.int32, (1, extent, 1), 1)
    top_mask = row_ids == 0
    bottom_mask = row_ids == extent - 1
    left_mask = col_ids == 0
    right_mask = col_ids == extent - 1
    target = target + jnp.where(top_mask, strips[..., 0, :, :][..., None, :, :], 0.0)
    target = target + jnp.where(right_mask, strips[..., 1, :, :][..., :, None, :], 0.0)
    target = target + jnp.where(bottom_mask, strips[..., 2, ::-1, :][..., None, :, :], 0.0)
    target = target + jnp.where(left_mask, strips[..., 3, ::-1, :][..., :, None, :], 0.0)
    target = target + jnp.where(top_mask & left_mask, points[..., 0, :][..., None, None, :], 0.0)
    target = target + jnp.where(top_mask & right_mask, points[..., 1, :][..., None, None, :], 0.0)
    target = target + jnp.where(
        bottom_mask & right_mask, points[..., 2, :][..., None, None, :], 0.0
    )
    target = target + jnp.where(bottom_mask & left_mask, points[..., 3, :][..., None, None, :], 0.0)
    return target


def forward_backward(
    padded, blocks, grad_out, dw_weight, norm_gain, w_in, bias_in, w_out, layer_scale
):
    extent = blocks.shape[-2]
    channels = blocks.shape[-1]
    mixed_cells = jnp.zeros(blocks.shape, jnp.float32)
    for row_off in range(3):
        for col_off in range(3):
            tap_index = 3 * row_off + col_off
            window = padded[..., row_off : row_off + extent, col_off : col_off + extent, :].astype(
                jnp.float32
            )
            mixed_cells = mixed_cells + window * dw_weight[:, tap_index]
    average = jnp.mean(mixed_cells, axis=-1, keepdims=True)
    centred = mixed_cells - average
    inv_std = lax.rsqrt(jnp.mean(centred * centred, axis=-1, keepdims=True) + 1e-06)
    standard = centred * inv_std
    normed = (standard * norm_gain).astype(jnp.bfloat16).reshape(-1, channels)
    hidden_pre = jnp.dot(normed, w_in, preferred_element_type=jnp.float32) + bias_in
    activated = jax.nn.gelu(hidden_pre, approximate=False).astype(jnp.bfloat16)
    branch = jnp.dot(activated, w_out, preferred_element_type=jnp.float32)
    cotangent = grad_out.reshape(-1, channels).astype(jnp.float32)
    block_out = (
        (blocks.reshape(-1, channels).astype(jnp.float32) + layer_scale * branch)
        .astype(jnp.bfloat16)
        .reshape(blocks.shape)
    )
    grad_scale = jnp.sum(cotangent * branch, axis=0)
    grad_mix = (cotangent * layer_scale).astype(jnp.bfloat16)
    grad_w_out = lax.dot_general(
        activated, grad_mix, (((0,), (0,)), ((), ())), preferred_element_type=jnp.float32
    )
    grad_act = lax.dot_general(
        grad_mix, w_out, (((1,), (1,)), ((), ())), preferred_element_type=jnp.float32
    )
    gelu_slope = (
        0.5 * (1.0 + lax.erf(hidden_pre * INV_ROOT_TWO))
        + hidden_pre * jnp.exp(-0.5 * hidden_pre * hidden_pre) * INV_ROOT_TAU
    )
    grad_hidden = (grad_act * gelu_slope).astype(jnp.bfloat16)
    grad_bias = jnp.sum(grad_hidden.astype(jnp.float32), axis=0)
    grad_w_in = lax.dot_general(
        normed, grad_hidden, (((0,), (0,)), ((), ())), preferred_element_type=jnp.float32
    )
    grad_normed = lax.dot_general(
        grad_hidden, w_in, (((1,), (1,)), ((), ())), preferred_element_type=jnp.float32
    ).reshape(blocks.shape)
    grad_gain = jnp.sum((grad_normed * standard).reshape(-1, channels), axis=0)
    grad_unit = grad_normed * norm_gain
    grad_mixed = (
        grad_unit
        - jnp.mean(grad_unit, axis=-1, keepdims=True)
        - standard * jnp.mean(grad_unit * standard, axis=-1, keepdims=True)
    ) * inv_std
    pad_widths = [(0, 0)] * (grad_mixed.ndim - 3) + [(2, 2), (2, 2), (0, 0)]
    wide_grad = jnp.pad(grad_mixed, pad_widths)
    grad_padded = jnp.zeros(padded.shape, jnp.float32)
    dw_columns = []
    for row_off in range(3):
        for col_off in range(3):
            tap_index = 3 * row_off + col_off
            window = padded[..., row_off : row_off + extent, col_off : col_off + extent, :].astype(
                jnp.float32
            )
            shifted = wide_grad[
                ..., 2 - row_off : 4 - row_off + extent, 2 - col_off : 4 - col_off + extent, :
            ]
            grad_padded = grad_padded + shifted * dw_weight[:, tap_index]
            dw_columns.append(jnp.sum((grad_mixed * window).reshape(-1, channels), axis=0))
    grad_dw = jnp.stack(dw_columns, axis=1)
    return (
        block_out,
        grad_padded,
        (grad_dw, grad_gain, grad_w_in, grad_bias, grad_w_out, grad_scale),
    )


def body(
    inputs,
    grad_out,
    seam_links,
    corner_links,
    dw_weight,
    norm_gain,
    w_in,
    bias_in,
    w_out,
    layer_scale,
):
    all_strips, all_points = (
        lax.all_gather(edge_strips(inputs), "tile", axis=1, tiled=True),
        lax.all_gather(corner_cells(inputs), "tile", axis=1, tiled=True),
    )
    strips, points = fetch_linked(all_strips, all_points, seam_links, corner_links)
    padded = assemble(inputs, strips, points)
    block_out, grad_padded, partials = forward_backward(
        padded, inputs, grad_out, dw_weight, norm_gain, w_in, bias_in, w_out, layer_scale
    )
    grad_dw, grad_gain, grad_w_in, grad_bias, grad_w_out, grad_scale = partials
    interior, back_strips, back_points = padded_parts(grad_padded)
    home_strips, home_points = (
        lax.all_gather(back_strips.astype(jnp.bfloat16), "tile", axis=1, tiled=True).astype(
            back_strips.dtype
        ),
        lax.all_gather(back_points.astype(jnp.bfloat16), "tile", axis=1, tiled=True).astype(
            back_points.dtype
        ),
    )
    return_strips, return_points = fetch_linked(home_strips, home_points, seam_links, corner_links)
    x_grad = add_to_rims(grad_out.astype(jnp.float32) + interior, return_strips, return_points)
    cell_total = (
        lax.axis_size("tile")
        * lax.axis_size("rep")
        * inputs.shape[0]
        * inputs.shape[1]
        * inputs.shape[2]
        * inputs.shape[3]
    )
    factor = 1.0 / math.sqrt(cell_total)
    summed = lax.psum(
        (grad_dw, grad_gain, grad_w_in, grad_bias, grad_w_out, grad_scale), ("tile", "rep")
    )
    return (
        block_out,
        x_grad,
        summed[0] * factor,
        summed[1] * factor,
        summed[2] * factor,
        summed[3] * factor,
        summed[4] * factor,
        summed[5] * factor,
    )


def solution(mesh):
    placed = (
        P("rep", "tile", None, None, None),
        P("rep", "tile", None, None, None),
        P("tile", None, None),
        P("tile", None, None),
        P(),
        P(),
        P(),
        P(),
        P(),
        P(),
    )
    return jax.shard_map(
        body,
        mesh=mesh,
        in_specs=placed,
        out_specs=(
            P("rep", "tile", None, None, None),
            P("rep", "tile", None, None, None),
            P(),
            P(),
            P(),
            P(),
            P(),
            P(),
        ),
        check_vma=False,
    )
```

profile of v0, /device:TPU:0, one launch (start us, length us, event | category | flops | bytes accessed | tf_op | source)
XLA Modules:
  0.0 216.6 jit_solution(4268885214619424398)
XLA Ops:
  8.1 1.1 fusion.75
  11.5 6.2 %all_gather.12 = bf16[1,8,4,256]{3,2,0,1:T(4,128)(2,1)S(1)} all-gather(bf16[1,2,4,256]{3,2,0,1:T(4,128)(2,1)S(1)} %copy.212), channel_id=1, replica_groups=mesh['tile'=4,'rep'=8] {'tile'}, dimensions={1}, use_global_device_ids=true | all-gather | bytes 20480 | tf_op jit(solution)/shard_map/all_gather | solution.py:183
  19.4 7.6 %all_gather.13 = bf16[1,8,4,32,256]{4,3,1,2,0:T(8,128)(2,1)S(1)} all-gather(bf16[1,2,4,32,256]{4,3,1,2,0:T(8,128)(2,1)S(1)} %pad_maximum_fusion.3), channel_id=1, replica_groups=mesh['tile'=4,'rep'=8] {'tile'}, dimensions={1}, use_global_device_ids=true | all-gather | bytes 655360 | tf_op jit(solution)/shard_map/all_gather | solution.py:182
  28.4 1.7 maximum_maximum_fusion
  30.1 5.2 %fusion.72 = (f32[2,32,32]{2,1,0:T(8,128)S(1)}, f32[1,2,32,32,256]{4,3,2,1,0:T(8,128)S(1)}) fusion(f32[256]{0:T(256)S(1)} %bitcast.170, bf16[1,2,33,34,256]{4,3,2,1,0:T(8,128)(2,1)S(1)} %get-tuple-element.81, f32[256]{0:T(256)S(1)} %bitcast.172, f32[256]{0:T(256)S(1)} %bitcast.158, f32[256]{0:T(256)S(1)} %bitcast.160, ...), kind=kLoop, calls=%fused_computation.185 | loop fusion | flops 17299456 | bytes 9520128 | tf_op jit(solution)/shard_map/reduce_sum | solution.py:105
  36.8 19.3 %fusion.2 = (bf16[2048,1024]{1,0:T(8,128)(2,1)S(1)}, f32[2048,1024]{1,0:T(8,128)S(1)}) fusion(f32[1024]{0:T(1024)S(1)} %copy-done.13, bf16[2048,256]{1,0:T(8,128)(2,1)S(1)} %bitcast.144, bf16[256,1024]{1,0:T(8,128)(2,1)S(1)} %copy-done), kind=kOutput, calls=%fused_computation.8 | convolution fusion | flops 1212153856 | bytes 14159872 | tf_op jit(solution)/shard_map/dot_general | solution.py:110
  56.2 3.1 %fusion.58 = (f32[256]{0:T(256)}, bf16[2048,256]{1,0:T(8,128)(2,1)}, bf16[2048,256]{1,0:T(8,128)(2,1)S(1)}) fusion(bf16[1,2,32,32,256]{4,3,2,1,0:T(8,128)(2,1)S(1)} %copy-done.6, f32[256]{0:T(256)S(1)} %copy-done.14, bf16[1,2,32,32,256]{4,3,2,1,0:T(8,128)(2,1)S(1)} %copy-done.5, bf16[2048,1024]{1,0:T(8,128)(2,1)S(1)} %get-tuple-element.122, ...), kind=kOutput, calls=%fused_computation.102 | convolution fusion | flops 1078460160 | bytes 8914944 | tf_op jit(solution)/shard_map/dot_general | solution.py:112
  59.3 2.2 %fusion.82 = f32[1024,256]{1,0:T(8,128)} fusion(bf16[2048,1024]{1,0:T(8,128)(2,1)S(1)} %get-tuple-element.122, bf16[2048,256]{1,0:T(8,128)(2,1)S(1)} %get-tuple-element.82), kind=kOutput, calls=%fused_computation.194 | convolution fusion | flops 1073741824 | bytes 6291456 | tf_op jit(solution)/shard_map/dot_general | solution.py:121
  61.5 4.9 %convert_reduce_fusion = (f32[1024]{0:T(1024)S(1)}, bf16[2048,1024]{1,0:T(8,128)(2,1)S(1)}) fusion(f32[2048,1024]{1,0:T(8,128)S(1)} %get-tuple-element.123, f32[1024]{0:T(1024)S(1)} %copy-done.13, bf16[2048,256]{1,0:T(8,128)(2,1)S(1)} %get-tuple-element.82, bf16[1024,256]{1,0:T(8,128)(2,1)S(1)} %copy-done.12), kind=kOutput, calls=%fused_computation.15 | convolution fusion | flops 1101003776 | bytes 14163968 | tf_op jit(solution)/shard_map/dot_general | solution.py:124
  66.4 1.9 copy-done.15
  68.3 2.2 %fusion.81 = f32[256,1024]{1,0:T(8,128)} fusion(bf16[2048,256]{1,0:T(8,128)(2,1)S(1)} %bitcast.145, bf16[2048,1024]{1,0:T(8,128)(2,1)S(1)} %get-tuple-element.127), kind=kOutput, calls=%fused_computation.193 | convolution fusion | flops 1073741824 | bytes 6291456 | tf_op jit(solution)/shard_map/dot_general | solution.py:133
  70.6 3.6 %multiply_reduce_fusion.3 = (f32[2048]{0:T(1024)S(1)}, f32[2048,256]{1,0:T(8,128)S(1)}) fusion(f32[256]{0:T(256)S(1)} %copy-done.9, bf16[2048,1024]{1,0:T(8,128)(2,1)} %copy-done.15, bf16[256,1024]{1,0:T(8,128)(2,1)S(1)} %copy-done), kind=kOutput, calls=%fused_computation.109 | convolution fusion | flops 1074788352 | bytes 6824960 | tf_op jit(solution)/shard_map/dot_general | solution.py:136
  74.2 1.1 multiply_reduce_fusion
  75.6 8.3 %fusion.48 = (f32[256]{0:T(256)S(1)}, f32[256]{0:T(256)S(1)}, f32[256]{0:T(256)S(1)}, f32[256]{0:T(256)S(1)}, f32[256]{0:T(256)S(1)}, /*index=5*/f32[256]{0:T(25...) fusion(bf16[1,2,33,34,256]{4,3,2,1,0:T(8,128)(2,1)} %copy-done.2, ...), kind=kLoop, calls=%fused_computation.89 | loop fusion | flops 20969216 | bytes 13740032 | tf_op jit(solution)/shard_map/reduce_sum | solution.py:160
  83.9 2.8 %fusion.24 = f32[1,2,34,34,256]{4,3,2,1,0:T(8,128)S(1)} fusion(f32[1,2,32,32,256]{4,3,2,1,0:T(8,128)S(1)} %get-tuple-element.71, f32[256]{0:T(256)S(1)} %bitcast.171, f32[256]{0:T(256)S(1)} %bitcast.173, f32[256]{0:T(256)S(1)} %bitcast.159, f32[256]{0:T(256)S(1)} %bitcast.161, f32[256]{0:T(256)S(1)} %bitcast.163, f32[256]{0:T(256)S(1)} %bitcast.165, ...), kind=kLoop, calls=%fused_computation.48 | loop fusion | flops 10061824 | bytes 4473856 | tf_op jit(solution)/shard_map/add | solution.py:159
  88.7 40.9 %all-reduce.1 = (f32[256,9]{0,1:T(8,128)}, f32[256]{0:T(256)S(1)}, f32[1024]{0:T(1024)S(1)}, f32[256]{0:T(256)S(1)}) all-reduce(f32[256,9]{0,1:T(8,128)S(1)} %stack.78, f32[256]{0:T(256)S(1)} %get-tuple-element.57, f32[1024]{0:T(1024)S(1)} %get-tuple-element.126, ...), channel_id=1, replica_groups=mesh['tile'=4,'rep'=8] {'tile','rep'}, use_global_device_ids=true, to_apply=%region_13.14 | all-reduce | flops 3840 | bytes 30720 | tf_op jit(solution)/shard_map/psum | solution.py:211
  132.4 8.5 %all_gather.14 = bf16[1,8,4,32,256]{4,3,2,0,1:T(8,128)(2,1)S(1)} all-gather(bf16[1,2,4,32,256]{4,3,2,0,1:T(8,128)(2,1)S(1)} %copy.228), channel_id=1, replica_groups=mesh['tile'=4,'rep'=8] {'tile'}, dimensions={1}, use_global_device_ids=true | all-gather | bytes 655360 | tf_op jit(solution)/shard_map/all_gather | solution.py:193
  142.0 2.5 %gather_fusion.2 = f32[8,32,256]{2,1,0:T(8,128)} fusion(f32[8,4,32,256]{3,2,1,0:T(8,128)} %bitcast_convert_fusion, s32[8]{0:T(128)S(1)} %reshape.484), kind=kCustom, calls=%fused_computation.2 | custom fusion | bytes 524352 | tf_op jit(solution)/shard_map/gather | solution.py:32
  144.5 1.6 rev.37
  146.1 1.1 broadcast_select_fusion
  148.6 5.2 %all_gather.15 = bf16[1,8,4,256]{3,2,0,1:T(4,128)(2,1)S(1)} all-gather(bf16[1,2,4,256]{3,2,0,1:T(4,128)(2,1)S(1)} %copy.230), channel_id=1, replica_groups=mesh['tile'=4,'rep'=8] {'tile'}, dimensions={1}, use_global_device_ids=true | all-gather | bytes 20480 | tf_op jit(solution)/shard_map/all_gather | solution.py:196
  156.0 4.5 %fusion.56 = f32[1,2,32,32,256]{4,3,2,1,0:T(8,128)} fusion(f32[1,2,34,34,256]{4,3,2,1,0:T(8,128)S(1)} %fusion.24, bf16[1,2,32,32,256]{4,3,2,1,0:T(8,128)(2,1)} %param.11, f32[2,256]{1,0:T(2,128)S(1)} %bitcast.174, f32[2,256]{1,0:T(2,128)S(1)} %bitcast.175, f32[2,256]{1,0:T(2,128)S(1)} %bitcast.176, f32[2,256]{1,0:T(2,128)S(1)} %bitcast.177, ...), kind=kLoop, calls=%fused_computation.98 | loop fusion | flops 9437184 | bytes 5531648 | tf_op jit(solution)/shard_map/add | solution.py:88
  160.5 45.8 %all-reduce.5.cloned.1.call-done = (f32[256,1024]{1,0:T(8,128)}, f32[1024,256]{1,0:T(8,128)}) async-done(((f32[256,1024]{1,0:T(8,128)}, f32[1024,256]{1,0:T(8,128)}), (f32[256,1024]{1,0:T(8,128)}, f32[1024,256]{1,0:T(8,128)})) %all-reduce.5.cloned.1.call-update) | async-done | bytes 2097168 | tf_op jit(solution)/shard_map/psum | solution.py:211
  206.3 2.4 %broadcast_multiply_fusion = f32[1024,256]{1,0:T(8,128)} fusion(f32[1024,256]{1,0:T(8,128)} %get-tuple-element.70), kind=kLoop, calls=%fused_computation.118 | loop fusion | flops 262144 | bytes 2097152 | tf_op jit(solution)/shard_map/mul | solution.py:221
  (109 shorter events, 18.1 us)
Async XLA Ops:
  7.2 29.6 %copy-start = (bf16[256,1024]{1,0:T(8,128)(2,1)S(1)}, bf16[256,1024]{1,0:T(8,128)(2,1)}, u32[]{:S(2)}) copy-start(bf16[256,1024]{1,0:T(8,128)(2,1)} %param.16) | copy-start | bytes 1572868
  7.2 21.2 %copy-start.4 = (bf16[1,2,32,32,256]{4,3,2,1,0:T(8,128)(2,1)S(1)}, bf16[1,2,32,32,256]{4,3,2,1,0:T(8,128)(2,1)}, u32[]{:S(2)}) copy-start(bf16[1,2,32,32,256]{4,3,2,1,0:T(8,128)(2,1)} %param.10) | copy-start | bytes 3145732
  7.2 21.1 %copy-start.10 = (f32[256,9]{0,1:T(8,128)S(1)}, f32[256,9]{0,1:T(8,128)}, u32[]{:S(2)}) copy-start(f32[256,9]{0,1:T(8,128)} %param.14) | copy-start | bytes 27652
  7.2 199.1 %all-reduce.5.cloned.1.call-start = ((), (), s32[]{:S(2)}) async-start(), calls=%async_computation | async-start | bytes 4194304 | tf_op jit(solution)/shard_map/psum | solution.py:211
  11.4 16.4 %copy-start.11 = (pred[2,4]{1,0:T(4,128)(4,1)}, pred[2,4]{1,0:T(4,128)(4,1)S(1)}, u32[]{:S(2)}) copy-start(pred[2,4]{1,0:T(4,128)(4,1)S(1)} %compare_bitcast_fusion) | copy-start | bytes 28
  30.1 5.2 %copy-start.1 = (bf16[1,2,33,34,256]{4,3,2,1,0:T(8,128)(2,1)}, bf16[1,2,33,34,256]{4,3,2,1,0:T(8,128)(2,1)S(1)}, u32[]{:S(2)}) copy-start(bf16[1,2,33,34,256]{4,3,2,1,0:T(8,128)(2,1)S(1)} %get-tuple-element.80) | copy-start | bytes 3446788
  30.1 5.2 %copy-start.2 = (bf16[1,2,33,34,256]{4,3,2,1,0:T(8,128)(2,1)}, bf16[1,2,33,34,256]{4,3,2,1,0:T(8,128)(2,1)S(1)}, u32[]{:S(2)}) copy-start(bf16[1,2,33,34,256]{4,3,2,1,0:T(8,128)(2,1)S(1)} %get-tuple-element.81) | copy-start | bytes 3446788
  30.1 5.9 %copy-start.9 = (f32[256]{0:T(256)S(1)}, f32[256]{0:T(256)}, u32[]{:S(2)}) copy-start(f32[256]{0:T(256)} %param.15) | copy-start | bytes 3076
  35.3 1.4 copy-start.13
  36.8 19.4 %copy-start.5 = (bf16[1,2,32,32,256]{4,3,2,1,0:T(8,128)(2,1)S(1)}, bf16[1,2,32,32,256]{4,3,2,1,0:T(8,128)(2,1)}, u32[]{:S(2)}) copy-start(bf16[1,2,32,32,256]{4,3,2,1,0:T(8,128)(2,1)} %param.10) | copy-start | bytes 3145732
  36.8 19.4 %copy-start.6 = (bf16[1,2,32,32,256]{4,3,2,1,0:T(8,128)(2,1)S(1)}, bf16[1,2,32,32,256]{4,3,2,1,0:T(8,128)(2,1)}, u32[]{:S(2)}) copy-start(bf16[1,2,32,32,256]{4,3,2,1,0:T(8,128)(2,1)} %param.11) | copy-start | bytes 3145732
  36.8 19.4 %copy-start.12 = (bf16[1024,256]{1,0:T(8,128)(2,1)S(1)}, bf16[1024,256]{1,0:T(8,128)(2,1)}, u32[]{:S(2)}) copy-start(bf16[1024,256]{1,0:T(8,128)(2,1)} %param.18) | copy-start | bytes 1572868
  36.8 19.4 %copy-start.14 = (f32[256]{0:T(256)S(1)}, f32[256]{0:T(256)}, u32[]{:S(2)}) copy-start(f32[256]{0:T(256)} %param.19) | copy-start | bytes 3076
  66.4 1.9 copy-start.15
  74.2 1.3 copy-start.3
  132.3 23.1 %copy-start.8 = (f32[256,9]{0,1:T(8,128)S(1)}, f32[256,9]{0,1:T(8,128)}, u32[]{:S(2)}) copy-start(f32[256,9]{0,1:T(8,128)} %get-tuple-element.65) | copy-start | bytes 27652
  206.3 2.4 %copy-start.7 = (f32[256,1024]{1,0:T(8,128)S(1)}, f32[256,1024]{1,0:T(8,128)}, u32[]{:S(2)}) copy-start(f32[256,1024]{1,0:T(8,128)} %get-tuple-element.69) | copy-start | bytes 3145732
Sparse Core Ops, SparseCore 0:
  70.7 135.4 all-reduce.4
where the time goes:
time: 217 us
  blocking collectives  68.5 us (32%)
  waiting for transfers between devices  45.8 us (21%)
  other arithmetic  35.4 us (16%)
  matrix products  35.4 us (16%)
  local copies, waits for them, and re-layouts  16.8 us (8%)
  between operations  14.6 us (7%)
    psum x1, waiting for transfers between devices, body(): lax.psum((grad_dw, grad_gain, grad_w_in, grad_bias, grad_w_out, grad_scal...  45.8 us
    psum x1, blocking collectives, body(): lax.psum((grad_dw, grad_gain, grad_w_in, grad_bias, grad_w_out, grad_scal...  40.9 us
    dot_general x1, matrix products, forward_backward(): jnp.dot(normed, w_in, preferred_element_type=jnp.float32) + bias_in  19.3 us
    all_gather x1, blocking collectives, body(): lax.all_gather(back_strips.astype(jnp.bfloat16), 'tile', axis=1, tiled=True)  8.53 us
    reduce_sum x1, other arithmetic, forward_backward(): jnp.sum((grad_mixed * window).reshape(-1, channels), axis=0)  8.32 us
    all_gather x1, blocking collectives, body(): lax.all_gather(edge_strips(inputs), 'tile', axis=1, tiled=True)  7.62 us
    all_gather x1, blocking collectives, body(): lax.all_gather(corner_cells(inputs), 'tile', axis=1, tiled=True)  6.22 us
    all_gather x1, blocking collectives, body(): lax.all_gather(back_points.astype(jnp.bfloat16), 'tile', axis=1, tiled=True)  5.19 us
  transfers between devices with their start and end apart: 1, of which 1 were waited for; matrix products, arithmetic and copies ran while one was open for 16% of the time, Pallas kernels for 0%

commit v1 on v0

--- a/solution.py
+++ b/solution.py
@@ -209,7 +209,7 @@
     )
     factor = 1.0 / math.sqrt(cell_total)
     summed = lax.psum(
-        (grad_dw, grad_gain, grad_w_in, grad_bias, grad_w_out, grad_scale), ("tile", "rep")
+        lax.psum((grad_dw, grad_gain, grad_w_in, grad_bias, grad_w_out, grad_scale), "rep"), "tile"
     )
     return (
         block_out,

time: 217 us -> 240 us (1.11)
  waiting for transfers between devices: 45.8 us -> 60.4 us
  blocking collectives: 68.5 us -> 75.3 us
    psum x0 -> x1, waiting for transfers between devices: none -> 47.7 us  [body(): lax.psum(lax.psum((grad_dw, grad_gain, grad_w_in, grad_bias, grad_w_out,...]
    psum x1, waiting for transfers between devices: 45.8 us -> 12.7 us  [body(): lax.psum((grad_dw, grad_gain, grad_w_in, grad_bias, grad_w_out, grad_scal...]
    psum x0 -> x1, blocking collectives: none -> 10.6 us  [body(): lax.psum(lax.psum((grad_dw, grad_gain, grad_w_in, grad_bias, grad_w_out,...]
    psum x1, blocking collectives: 40.9 us -> 38.4 us  [body(): lax.psum((grad_dw, grad_gain, grad_w_in, grad_bias, grad_w_out, grad_scal...]
  transfers between devices with their start and end apart: 1 -> 2, of which waited for: 1 -> 2; matrix products, arithmetic and copies ran while one was open for 16% -> 14% of each run, Pallas kernels for 0% -> 0%
where the time goes in v1:
time: 240 us; the launch traced here: 239 us
  blocking collectives  75.3 us (31%)
  waiting for transfers between devices  60.4 us (25%)
  matrix products  36 us (15%)
  other arithmetic  35.3 us (15%)
  local copies, waits for them, and re-layouts  17.5 us (7%)
  between operations  14.7 us (6%)
    psum x1, waiting for transfers between devices, body(): lax.psum(lax.psum((grad_dw, grad_gain, grad_w_in, grad_bias, grad_w_out,...  47.7 us
    psum x1, blocking collectives, body(): lax.psum((grad_dw, grad_gain, grad_w_in, grad_bias, grad_w_out, grad_scal...  38.4 us
    dot_general x1, matrix products, forward_backward(): jnp.dot(normed, w_in, preferred_element_type=jnp.float32) + bias_in  19.3 us
    psum x1, waiting for transfers between devices, body(): lax.psum((grad_dw, grad_gain, grad_w_in, grad_bias, grad_w_out, grad_scal...  12.7 us
    psum x1, blocking collectives, body(): lax.psum(lax.psum((grad_dw, grad_gain, grad_w_in, grad_bias, grad_w_out,...  10.6 us
    reduce_sum x1, other arithmetic, forward_backward(): jnp.sum((grad_mixed * window).reshape(-1, channels), axis=0)  8.94 us
    all_gather x1, blocking collectives, body(): lax.all_gather(edge_strips(inputs), 'tile', axis=1, tiled=True)  7.62 us
    all_gather x1, blocking collectives, body(): lax.all_gather(back_strips.astype(jnp.bfloat16), 'tile', axis=1, tiled=True)  7.29 us
  transfers between devices with their start and end apart: 2, of which 2 were waited for; matrix products, arithmetic and copies ran while one was open for 14% of the time, Pallas kernels for 0%

profile of v1, /device:TPU:0, one launch (start us, length us, event | category | flops | bytes accessed | tf_op | source)
XLA Modules:
  0.0 239.2 jit_solution(7799515082291476928)
XLA Ops:
  8.1 1.1 fusion.75
  11.5 6.2 %all_gather.12 = bf16[1,8,4,256]{3,2,0,1:T(4,128)(2,1)S(1)} all-gather(bf16[1,2,4,256]{3,2,0,1:T(4,128)(2,1)S(1)} %copy.212), channel_id=1, replica_groups=mesh['tile'=4,'rep'=8] {'tile'}, dimensions={1}, use_global_device_ids=true | all-gather | bytes 20480 | tf_op jit(solution)/shard_map/all_gather | solution.py:183
  19.4 7.6 %all_gather.13 = bf16[1,8,4,32,256]{4,3,1,2,0:T(8,128)(2,1)S(1)} all-gather(bf16[1,2,4,32,256]{4,3,1,2,0:T(8,128)(2,1)S(1)} %pad_maximum_fusion.3), channel_id=1, replica_groups=mesh['tile'=4,'rep'=8] {'tile'}, dimensions={1}, use_global_device_ids=true | all-gather | bytes 655360 | tf_op jit(solution)/shard_map/all_gather | solution.py:182
  28.4 1.7 maximum_maximum_fusion
  30.1 5.2 %fusion.72 = (f32[2,32,32]{2,1,0:T(8,128)S(1)}, f32[1,2,32,32,256]{4,3,2,1,0:T(8,128)S(1)}) fusion(f32[256]{0:T(256)S(1)} %bitcast.170, bf16[1,2,33,34,256]{4,3,2,1,0:T(8,128)(2,1)S(1)} %get-tuple-element.87, f32[256]{0:T(256)S(1)} %bitcast.172, f32[256]{0:T(256)S(1)} %bitcast.158, f32[256]{0:T(256)S(1)} %bitcast.160, ...), kind=kLoop, calls=%fused_computation.185 | loop fusion | flops 17299456 | bytes 9520128 | tf_op jit(solution)/shard_map/reduce_sum | solution.py:105
  36.8 19.3 %fusion.2 = (bf16[2048,1024]{1,0:T(8,128)(2,1)S(1)}, f32[2048,1024]{1,0:T(8,128)S(1)}) fusion(f32[1024]{0:T(1024)S(1)} %copy-done.13, bf16[2048,256]{1,0:T(8,128)(2,1)S(1)} %bitcast.144, bf16[256,1024]{1,0:T(8,128)(2,1)S(1)} %copy-done), kind=kOutput, calls=%fused_computation.8 | convolution fusion | flops 1212153856 | bytes 14159872 | tf_op jit(solution)/shard_map/dot_general | solution.py:110
  56.2 3.1 %fusion.58 = (f32[256]{0:T(256)}, bf16[2048,256]{1,0:T(8,128)(2,1)}, bf16[2048,256]{1,0:T(8,128)(2,1)S(1)}) fusion(bf16[1,2,32,32,256]{4,3,2,1,0:T(8,128)(2,1)S(1)} %copy-done.7, f32[256]{0:T(256)S(1)} %copy-done.14, bf16[1,2,32,32,256]{4,3,2,1,0:T(8,128)(2,1)S(1)} %copy-done.5, bf16[2048,1024]{1,0:T(8,128)(2,1)S(1)} %get-tuple-element.128, ...), kind=kOutput, calls=%fused_computation.102 | convolution fusion | flops 1078460160 | bytes 8914944 | tf_op jit(solution)/shard_map/dot_general | solution.py:112
  59.3 2.3 fusion.82
  61.6 5.5 %convert_reduce_fusion = (f32[1024]{0:T(1024)}, bf16[2048,1024]{1,0:T(8,128)(2,1)S(1)}) fusion(f32[2048,1024]{1,0:T(8,128)S(1)} %get-tuple-element.129, f32[1024]{0:T(1024)S(1)} %copy-done.13, bf16[2048,256]{1,0:T(8,128)(2,1)S(1)} %get-tuple-element.88, bf16[1024,256]{1,0:T(8,128)(2,1)S(1)} %copy-done.12), kind=kOutput, calls=%fused_computation.15 | convolution fusion | flops 1101003776 | bytes 14163968 | tf_op jit(solution)/shard_map/dot_general | solution.py:124
  67.0 1.9 copy-done.15
  69.0 2.2 fusion.81
  71.3 3.6 %multiply_reduce_fusion.3 = (f32[2048]{0:T(1024)S(1)}, f32[2048,256]{1,0:T(8,128)S(1)}) fusion(f32[256]{0:T(256)S(1)} %copy-done.9, bf16[2048,1024]{1,0:T(8,128)(2,1)} %copy-done.15, bf16[256,1024]{1,0:T(8,128)(2,1)S(1)} %copy-done), kind=kOutput, calls=%fused_computation.109 | convolution fusion | flops 1074788352 | bytes 6824960 | tf_op jit(solution)/shard_map/dot_general | solution.py:136
  76.3 8.9 %fusion.48 = (f32[256]{0:T(256)S(1)}, f32[256]{0:T(256)}, f32[256]{0:T(256)}, f32[256]{0:T(256)}, f32[256]{0:T(256)}, /*index=5*/f32[256]{0:T(256)}, f32[256]{0:...) fusion(bf16[1,2,33,34,256]{4,3,2,1,0:T(8,128)(2,1)} %copy-done.2, ...), kind=kLoop, calls=%fused_computation.89 | loop fusion | flops 20969216 | bytes 13740032 | tf_op jit(solution)/shard_map/reduce_sum | solution.py:160
  85.2 2.7 %fusion.24 = f32[1,2,34,34,256]{4,3,2,1,0:T(8,128)S(1)} fusion(f32[1,2,32,32,256]{4,3,2,1,0:T(8,128)S(1)} %get-tuple-element.77, f32[256]{0:T(256)S(1)} %bitcast.171, f32[256]{0:T(256)S(1)} %bitcast.173, f32[256]{0:T(256)S(1)} %bitcast.159, f32[256]{0:T(256)S(1)} %bitcast.161, f32[256]{0:T(256)S(1)} %bitcast.163, f32[256]{0:T(256)S(1)} %bitcast.165, ...), kind=kLoop, calls=%fused_computation.48 | loop fusion | flops 10061824 | bytes 4473856 | tf_op jit(solution)/shard_map/add | solution.py:159
  90.1 7.3 %all_gather.14 = bf16[1,8,4,32,256]{4,3,2,0,1:T(8,128)(2,1)S(1)} all-gather(bf16[1,2,4,32,256]{4,3,2,0,1:T(8,128)(2,1)S(1)} %copy.228), channel_id=1, replica_groups=mesh['tile'=4,'rep'=8] {'tile'}, dimensions={1}, use_global_device_ids=true | all-gather | bytes 655360 | tf_op jit(solution)/shard_map/all_gather | solution.py:193
  98.4 2.5 %gather_fusion.2 = f32[8,32,256]{2,1,0:T(8,128)} fusion(f32[8,4,32,256]{3,2,1,0:T(8,128)} %bitcast_convert_fusion, s32[8]{0:T(128)S(1)} %reshape.484), kind=kCustom, calls=%fused_computation.2 | custom fusion | bytes 524352 | tf_op jit(solution)/shard_map/gather | solution.py:32
  100.9 1.6 rev.37
  103.4 5.2 %all_gather.15 = bf16[1,8,4,256]{3,2,0,1:T(4,128)(2,1)S(1)} all-gather(bf16[1,2,4,256]{3,2,0,1:T(4,128)(2,1)S(1)} %copy.230), channel_id=1, replica_groups=mesh['tile'=4,'rep'=8] {'tile'}, dimensions={1}, use_global_device_ids=true | all-gather | bytes 20480 | tf_op jit(solution)/shard_map/all_gather | solution.py:196
  109.9 38.4 %all-reduce.1 = (f32[256,9]{0,1:T(8,128)S(1)}, f32[256]{0:T(256)S(1)}, f32[1024]{0:T(1024)S(1)}, f32[256]{0:T(256)S(1)}) all-reduce(f32[256,9]{0,1:T(8,128)S(1)} %stack.78, f32[256]{0:T(256)S(1)} %get-tuple-element.57, f32[1024]{0:T(1024)} %get-tuple-element.132, f32[256]{0:T(256)} %get-tuple-element.80), channel_id=1, replica_groups=mesh['tile'=4,'rep'=8] {'rep'}, use_global_device_ids=true, to_apply=%region_13.14 | all-reduce | flops 3840 | bytes 30720 | tf_op jit(solution)/shard_map/psum | solution.py:212
  148.3 10.6 %all-reduce.3 = (f32[256,9]{0,1:T(8,128)S(1)}, f32[256]{0:T(256)S(1)}, f32[1024]{0:T(1024)S(1)}, f32[256]{0:T(256)S(1)}) all-reduce(f32[256,9]{0,1:T(8,128)S(1)} %get-tuple-element.65, f32[256]{0:T(256)S(1)} %get-tuple-element.66, f32[1024]{0:T(1024)S(1)} %get-tuple-element.67, ...), channel_id=1, replica_groups=mesh['tile'=4,'rep'=8] {'tile'}, use_global_device_ids=true, to_apply=%region_14.15 | all-reduce | flops 3840 | bytes 30720 | tf_op jit(solution)/shard_map/psum | solution.py:211
  162.4 12.7 %all-reduce.8.cloned.1.call-done = (f32[256,1024]{1,0:T(8,128)}, f32[1024,256]{1,0:T(8,128)}) async-done(((f32[256,1024]{1,0:T(8,128)}, f32[1024,256]{1,0:T(8,128)}), (f32[256,1024]{1,0:T(8,128)}, f32[1024,256]{1,0:T(8,128)})) %all-reduce.8.cloned.1.call-update) | async-done | bytes 2097168 | tf_op jit(solution)/shard_map/psum | solution.py:212
  176.8 4.5 %fusion.56 = f32[1,2,32,32,256]{4,3,2,1,0:T(8,128)} fusion(f32[1,2,34,34,256]{4,3,2,1,0:T(8,128)S(1)} %fusion.24, bf16[1,2,32,32,256]{4,3,2,1,0:T(8,128)(2,1)} %param.11, f32[2,256]{1,0:T(2,128)S(1)} %bitcast.174, f32[2,256]{1,0:T(2,128)S(1)} %bitcast.175, f32[2,256]{1,0:T(2,128)S(1)} %bitcast.176, f32[2,256]{1,0:T(2,128)S(1)} %bitcast.177, ...), kind=kLoop, calls=%fused_computation.98 | loop fusion | flops 9437184 | bytes 5531648 | tf_op jit(solution)/shard_map/add | solution.py:88
  181.3 47.7 %all-reduce.10.cloned.1.call-done = (f32[256,1024]{1,0:T(8,128)}, f32[1024,256]{1,0:T(8,128)}) async-done(((f32[256,1024]{1,0:T(8,128)}, f32[1024,256]{1,0:T(8,128)}), (f32[256,1024]{1,0:T(8,128)}, f32[1024,256]{1,0:T(8,128)})) %all-reduce.10.cloned.1.call-update) | async-done | bytes 2097168 | tf_op jit(solution)/shard_map/psum | solution.py:211
  229.0 2.4 broadcast_multiply_fusion
  (113 shorter events, 20.3 us)
Async XLA Ops:
  7.2 29.6 %copy-start = (bf16[256,1024]{1,0:T(8,128)(2,1)S(1)}, bf16[256,1024]{1,0:T(8,128)(2,1)}, u32[]{:S(2)}) copy-start(bf16[256,1024]{1,0:T(8,128)(2,1)} %param.16) | copy-start | bytes 1572868
  7.2 21.2 %copy-start.4 = (bf16[1,2,32,32,256]{4,3,2,1,0:T(8,128)(2,1)S(1)}, bf16[1,2,32,32,256]{4,3,2,1,0:T(8,128)(2,1)}, u32[]{:S(2)}) copy-start(bf16[1,2,32,32,256]{4,3,2,1,0:T(8,128)(2,1)} %param.10) | copy-start | bytes 3145732
  7.2 21.1 %copy-start.10 = (f32[256,9]{0,1:T(8,128)S(1)}, f32[256,9]{0,1:T(8,128)}, u32[]{:S(2)}) copy-start(f32[256,9]{0,1:T(8,128)} %param.14) | copy-start | bytes 27652
  7.2 167.9 %all-reduce.8.cloned.1.call-start = ((), (), s32[]{:S(2)}) async-start(), calls=%async_computation | async-start | bytes 4194304 | tf_op jit(solution)/shard_map/psum | solution.py:212
  11.4 18.7 %copy-start.11 = (pred[2,4]{1,0:T(4,128)(4,1)}, pred[2,4]{1,0:T(4,128)(4,1)S(1)}, u32[]{:S(2)}) copy-start(pred[2,4]{1,0:T(4,128)(4,1)S(1)} %compare_bitcast_fusion) | copy-start | bytes 28
  30.1 5.2 %copy-start.1 = (bf16[1,2,33,34,256]{4,3,2,1,0:T(8,128)(2,1)}, bf16[1,2,33,34,256]{4,3,2,1,0:T(8,128)(2,1)S(1)}, u32[]{:S(2)}) copy-start(bf16[1,2,33,34,256]{4,3,2,1,0:T(8,128)(2,1)S(1)} %get-tuple-element.86) | copy-start | bytes 3446788
  30.1 5.2 %copy-start.2 = (bf16[1,2,33,34,256]{4,3,2,1,0:T(8,128)(2,1)}, bf16[1,2,33,34,256]{4,3,2,1,0:T(8,128)(2,1)S(1)}, u32[]{:S(2)}) copy-start(bf16[1,2,33,34,256]{4,3,2,1,0:T(8,128)(2,1)S(1)} %get-tuple-element.87) | copy-start | bytes 3446788
  30.1 5.9 %copy-start.9 = (f32[256]{0:T(256)S(1)}, f32[256]{0:T(256)}, u32[]{:S(2)}) copy-start(f32[256]{0:T(256)} %param.15) | copy-start | bytes 3076
  35.3 1.4 copy-start.13
  36.8 19.4 %copy-start.5 = (bf16[1,2,32,32,256]{4,3,2,1,0:T(8,128)(2,1)S(1)}, bf16[1,2,32,32,256]{4,3,2,1,0:T(8,128)(2,1)}, u32[]{:S(2)}) copy-start(bf16[1,2,32,32,256]{4,3,2,1,0:T(8,128)(2,1)} %param.10) | copy-start | bytes 3145732
  36.8 19.4 %copy-start.7 = (bf16[1,2,32,32,256]{4,3,2,1,0:T(8,128)(2,1)S(1)}, bf16[1,2,32,32,256]{4,3,2,1,0:T(8,128)(2,1)}, u32[]{:S(2)}) copy-start(bf16[1,2,32,32,256]{4,3,2,1,0:T(8,128)(2,1)} %param.11) | copy-start | bytes 3145732
  36.8 19.4 %copy-start.12 = (bf16[1024,256]{1,0:T(8,128)(2,1)S(1)}, bf16[1024,256]{1,0:T(8,128)(2,1)}, u32[]{:S(2)}) copy-start(bf16[1024,256]{1,0:T(8,128)(2,1)} %param.18) | copy-start | bytes 1572868
  36.8 19.4 %copy-start.14 = (f32[256]{0:T(256)S(1)}, f32[256]{0:T(256)}, u32[]{:S(2)}) copy-start(f32[256]{0:T(256)} %param.19) | copy-start | bytes 3076
  67.0 1.9 copy-start.15
  71.2 157.7 %all-reduce.10.cloned.1.call-start = ((), (), s32[]{:S(2)}) async-start(), calls=%async_computation.1 | async-start | bytes 4194304 | tf_op jit(solution)/shard_map/psum | solution.py:211
  74.9 1.3 copy-start.3
  88.6 1.1 copy-start.6
  228.9 2.4 copy-start.8
Sparse Core Ops, SparseCore 0:
  71.4 103.7 all-reduce.7
  177.6 51.3 all-reduce.9
